TPU v7x, 512 devices: a whole 4x8x8 slice. The times are simulated.
512 devices in a mesh: land: 128 (over y, z, core), cam: 4 (over x).
Axes of the slice: x: 4, y: 8, z: 8, core: 2. Of those that a mesh axis runs over, the one named last changes fastest.
Arguments:
- jac_cam: float32 [2, 15, 4, 262144], P(None, None, None, ('land', 'cam')), may hold values from -6 to 6
- jac_land: float32 [2, 3, 4, 262144], P(None, None, None, ('land', 'cam')), may hold values from -6 to 6
- land_damp: float32 [3, 262144], P(None, ('land', 'cam')), may hold values from 0.5 to 4
- obs_slot: int32 [4, 262144], P(None, ('land', 'cam')), may hold values from 0 to 4095
- tile_count: int32 [512], P(('land', 'cam')), may hold values from 1 to 4, as said below
- send_list: int32 [512, 4096], P(('land', 'cam')), may hold values from 0 to 1023
- rhs: float32 [15, 131072], P(None, ('land', 'cam')), may hold values from -6 to 6
- precond: float32 [15, 15, 131072], P(None, None, ('land', 'cam')), as said below
- cam_damp: float32 [15, 131072], P(None, ('land', 'cam')), may hold values from 0.5 to 4
Outputs:
- camera_step: float32 [15, 131072], P(None, ('land', 'cam'))
- residual: float32 [15, 131072], P(None, ('land', 'cam'))
Inputs may be any that keep to these rules, and one draw needn't show every extreme that they name: obs_slot[k, l] // 32 is the owner group of the observed camera and obs_slot[k, l] mod 32 its entry in that group's list for the observing device. `send_list`: entry i * 32 + e, with e < 32, of a device's row is a position among its land index's 1024 cameras, ordered by index on cam; the same camera may appear more than once. `tile_count`: some device holds 4 live tiles in every draw. `precond`: each camera's block is symmetric positive definite.
All inputs are finite; a program needn't handle non-finite values.
Results may differ from a plain program's by a relative error of at most 0.00055.
Values sent between devices are 32-bit elements; how exact they have to be, the bound alone decides.
A program may use at most 64 MiB of HBM per device.

v0:
```python
import jax
import jax.numpy as jnp
from jax import lax
from jax.sharding import PartitionSpec as P

PARAMS = 15
TILE = 128
ITERS = 2


def invert_three(matrix):
    adjugate = [[None, None, None], [None, None, None], [None, None, None]]
    for row_ix in range(3):
        for col_ix in range(3):
            next_row = (col_ix + 1) % 3
            last_row = (col_ix + 2) % 3
            next_col = (row_ix + 1) % 3
            last_col = (row_ix + 2) % 3
            adjugate[row_ix][col_ix] = (
                matrix[next_row][next_col] * matrix[last_row][last_col]
                - matrix[next_row][last_col] * matrix[last_row][next_col]
            )
    determinant = (
        matrix[0][0] * adjugate[0][0]
        + matrix[0][1] * adjugate[1][0]
        + matrix[0][2] * adjugate[2][0]
    )
    return [[adjugate[row_ix][col_ix] / determinant for col_ix in range(3)] for row_ix in range(3)]


def landmark_blocks(land_jacobian, land_damp):
    matrix = []
    for row_ix in range(3):
        entries = []
        for col_ix in range(3):
            entry = jnp.sum(land_jacobian[:, row_ix] * land_jacobian[:, col_ix], axis=(0, 1))
            if row_ix == col_ix:
                entry = entry + land_damp[row_ix]
            entries.append(entry)
        matrix.append(entries)
    return matrix


def apply_inverse(inverse, vector):
    return jnp.stack(
        [
            inverse[row_ix][0] * vector[0]
            + inverse[row_ix][1] * vector[1]
            + inverse[row_ix][2] * vector[2]
            for row_ix in range(3)
        ]
    )


def precondition(blocks, vector):
    return jnp.sum(blocks * vector[None], axis=1)


def local(jac_cam, jac_land, land_damp, obs_slot, tile_count, send_list, rhs, precond, cam_damp):
    lm_dev = jac_cam.shape[3]
    live = (jnp.arange(lm_dev, dtype=jnp.int32) // TILE < tile_count[0]).astype(jnp.float32)
    cam_jacobian = jac_cam * live
    land_jacobian = jac_land * live
    inverse = invert_three(landmark_blocks(land_jacobian, land_damp))
    targets = send_list[0]
    slot_count = targets.shape[0]
    owned = rhs.shape[1]
    group_size = owned * lax.axis_size("cam")
    flat_slots = obs_slot.reshape(-1)
    start, blocks, damping = (rhs, precond, cam_damp)

    def global_dots(terms):
        return lax.psum(jnp.stack(terms), ("land", "cam"))

    camera_step = jnp.zeros_like(start)
    residual = start
    smoothed = precondition(blocks, residual)
    direction = smoothed
    energy = global_dots([jnp.sum(residual * smoothed)])[0]
    for iteration in range(ITERS):
        operate_group_dirs = lax.all_gather(direction, "cam", axis=1, tiled=True)
        outgoing = jnp.take(operate_group_dirs, targets, axis=1)
        incoming = lax.all_to_all(outgoing, "land", split_axis=1, concat_axis=1, tiled=True)
        gathered = jnp.take(incoming, obs_slot, axis=1)
        predicted = jnp.sum(cam_jacobian * gathered[None], axis=1)
        land_rhs = jnp.sum(land_jacobian * predicted[:, None], axis=(0, 2))
        land_step = apply_inverse(inverse, land_rhs)
        misfit = predicted - jnp.sum(land_jacobian * land_step[None, :, None], axis=1)
        cam_terms = jnp.sum(cam_jacobian * misfit[:, None], axis=0)
        slot_terms = (
            jnp.zeros((PARAMS, slot_count), jnp.float32)
            .at[:, flat_slots]
            .add(cam_terms.reshape(PARAMS, -1))
        )
        returned = lax.all_to_all(slot_terms, "land", split_axis=1, concat_axis=1, tiled=True)
        product = (
            lax.psum_scatter(
                jnp.zeros((PARAMS, group_size), jnp.float32).at[:, targets].add(returned),
                "cam",
                scatter_dimension=1,
                tiled=True,
            )
            + damping * direction
        )
        stride = energy / global_dots([jnp.sum(direction * product)])[0]
        camera_step = camera_step + stride * direction
        residual = residual - stride * product
        smoothed = precondition(blocks, residual)
        energy_new = global_dots([jnp.sum(residual * smoothed)])[0]
        direction = smoothed + energy_new / energy * direction
        energy = energy_new
    return (camera_step, residual)


def solution(mesh):
    return jax.shard_map(
        local,
        mesh=mesh,
        in_specs=(
            P(None, None, None, ("land", "cam")),
            P(None, None, None, ("land", "cam")),
            P(None, ("land", "cam")),
            P(None, ("land", "cam")),
            P(("land", "cam")),
            P(("land", "cam"), None),
            P(None, ("land", "cam")),
            P(None, None, ("land", "cam")),
            P(None, ("land", "cam")),
        ),
        out_specs=(P(None, ("land", "cam")), P(None, ("land", "cam"))),
        check_vma=False,
    )
```

profile of v0, /device:TPU:1, one launch (start us, length us, event | category | flops | bytes accessed | tf_op | source)
XLA Modules:
  0.0 617.1 jit_solution(5852986275021348650)
XLA Ops:
  7.2 0.7 compare_and_fusion
  7.9 0.7 fusion.8
  8.6 1.0 multiply_reduce_fusion.5
  9.7 11.1 %all_gather.6 = f32[15,1024]{0,1:T(8,128)S(1)} all-gather(f32[15,256]{0,1:T(8,128)S(1)} %copy.83), channel_id=1, replica_groups=mesh['land'=128,'cam'=4] {'cam'}, dimensions={1}, use_global_device_ids=true | all-gather | bytes 76800 | tf_op jit(solution)/shard_map/all_gather | solution.py:81
  20.8 14.1 %gather_fusion = f32[4096,15]{1,0:T(8,128)} fusion(f32[15,1024]{0,1:T(8,128)S(1)} %all_gather.6, s32[4096]{0:T(1024)S(1)} %fusion.8), kind=kCustom, calls=%fused_computation.clone | custom fusion | bytes 507904 | tf_op jit(solution)/shard_map/jit(_take)/gather | solution.py:82
  34.9 3.6 broadcast_select_fusion.1
  38.5 0.8 copy.84
  39.4 1.2 reshape.303
  40.6 20.5 %all-to-all-start = ((f32[128,1,480]{2,1,0:T(1,128)}), f32[128,1,480]{2,1,0:T(1,128)S(1)}, u32[]{:S(2)}, u32[]{:S(2)}) async-start(f32[128,1,480]{2,1,0:T(1,128)} %reshape.303), calls=%async_computation | async-start | bytes 524288 | tf_op jit(solution)/shard_map/all_to_all | solution.py:83
  61.8 0.6 compare_select_fusion.1
  62.4 12.9 %all-to-all-done = f32[128,1,480]{2,1,0:T(1,128)S(1)} async-done(((f32[128,1,480]{2,1,0:T(1,128)}), f32[128,1,480]{2,1,0:T(1,128)S(1)}, u32[]{:S(2)}, u32[]{:S(2)}) %all-to-all-start) | async-done | bytes 245792 | tf_op jit(solution)/shard_map/all_to_all | solution.py:83
  75.3 0.5 broadcast.151
  75.8 1.2 reduce.6
  77.3 0.8 copy.85
  78.1 5.5 gather_fusion.1
  83.6 0.3 select_bitcast_fusion.1
  83.9 0.3 copy.86
  84.5 0.6 multiply_add_fusion.9
  85.1 0.6 multiply_add_fusion.8
  85.7 0.6 multiply_add_fusion.7
  86.4 0.4 copy.101
  86.8 12.1 %scatter_custom_fusion = f32[15,4096]{0,1:T(8,128)S(1)} fusion(s32[2048]{0:T(1024)} %bitcast.96, f32[2048,15]{1,0:T(8,128)S(1)} %bitcast.78, f32[]{:T(128)} %constant.26.clone.1), kind=kCustom, calls=%fused_computation.14 | custom fusion | flops 30720 | bytes 246272 | tf_op jit(solution)/shard_map/scatter-add | solution.py:93
  98.9 0.8 copy.88
  99.8 1.2 reshape.305
  101.0 7.0 %all-to-all-start.1 = ((f32[128,1,480]{2,1,0:T(1,128)}), f32[128,1,480]{2,1,0:T(1,128)S(1)}, u32[]{:S(2)}, u32[]{:S(2)}) async-start(f32[128,1,480]{2,1,0:T(1,128)} %reshape.305), calls=%async_computation.1 | async-start | bytes 524288 | tf_op jit(solution)/shard_map/all_to_all | solution.py:95
  108.2 14.1 %all-to-all-done.1 = f32[128,1,480]{2,1,0:T(1,128)S(1)} async-done(((f32[128,1,480]{2,1,0:T(1,128)}), f32[128,1,480]{2,1,0:T(1,128)S(1)}, u32[]{:S(2)}, u32[]{:S(2)}) %all-to-all-start.1) | async-done | bytes 245792 | tf_op jit(solution)/shard_map/all_to_all | solution.py:95
  122.3 1.2 reduce.7
  123.8 0.3 copy.89
  124.1 0.5 reshape.254
  124.6 0.6 copy.90
  125.3 22.5 %scatter_custom_fusion.1 = f32[15,1024]{0,1:T(8,128)S(1)} fusion(s32[4096]{0:T(1024)S(1)} %bitcast.91, f32[4096,15]{1,0:T(8,128)S(1)} %copy.90, f32[]{:T(128)} %constant.26.clone.1), kind=kCustom, calls=%fused_computation.18 | custom fusion | flops 61440 | bytes 61444 | tf_op jit(solution)/shard_map/scatter-add | solution.py:98
  147.7 0.8 copy.91
  148.6 16.7 %reduce-scatter.3.cloned.1.call-done = f32[15,256]{1,0:T(8,128)} async-done(((f32[15,1024]{1,0:T(8,128)}), f32[15,256]{1,0:T(8,128)}) %reduce-scatter.3.cloned.1.call-update) | async-done | bytes 15376 | tf_op jit(solution)/shard_map/reduce_scatter | solution.py:97
  165.3 1.4 multiply_reduce_fusion.12
  166.7 99.5 %all-reduce = (f32[1]{0:T(128)}, f32[1]{0:T(128)}) all-reduce(f32[1]{0:T(128)} %bitcast, f32[1]{0:T(128)} %bitcast.21), channel_id=1, replica_groups=mesh['land'=128,'cam'=4] {'land','cam'}, use_global_device_ids=true, to_apply=%region_2.3 | all-reduce | flops 2 | bytes 16 | tf_op jit(solution)/shard_map/psum | solution.py:73
  267.5 0.7 multiply_subtract_fusion.1
  268.3 0.6 multiply_reduce_fusion.11
  268.9 95.7 %psum.30 = f32[1]{0:T(128)} all-reduce(f32[1]{0:T(128)} %bitcast.23), channel_id=1, replica_groups=mesh['land'=128,'cam'=4] {'land','cam'}, use_global_device_ids=true, to_apply=%region_20.23 | all-reduce | flops 1 | bytes 8 | tf_op jit(solution)/shard_map/psum | solution.py:73
  366.0 9.0 %all_gather.7 = f32[15,1024]{1,0:T(8,128)S(1)} all-gather(f32[15,256]{1,0:T(8,128)S(1)} %multiply_add_fusion.2), channel_id=1, replica_groups=mesh['land'=128,'cam'=4] {'cam'}, dimensions={1}, use_global_device_ids=true | all-gather | bytes 76800 | tf_op jit(solution)/shard_map/all_gather | solution.py:81
  375.2 14.1 %gather_fusion.2 = f32[4096,15]{1,0:T(8,128)} fusion(f32[15,1024]{0,1:T(8,128)S(1)} %copy.92, s32[4096]{0:T(1024)S(1)} %fusion.8), kind=kCustom, calls=%fused_computation.2.clone | custom fusion | bytes 507904 | tf_op jit(solution)/shard_map/jit(_take)/gather | solution.py:82
  389.3 3.6 broadcast_select_fusion
  392.9 0.8 copy.93
  393.8 0.5 reshape.307
  394.3 27.7 %all_to_all.48 = f32[128,1,480]{2,1,0:T(1,128)S(1)} all-to-all(f32[128,1,480]{2,1,0:T(1,128)S(1)} %reshape.307), channel_id=1, replica_groups=mesh['land'=128,'cam'=4] {'land'}, dimensions={0} | all-to-all | bytes 491520 | tf_op jit(solution)/shard_map/all_to_all | solution.py:83
  422.0 1.2 reduce.8
  423.5 0.8 copy.94
  424.3 5.5 gather_fusion.3
  429.8 0.3 select_bitcast_fusion
  430.2 0.3 copy.95
  430.8 0.4 copy.102
  431.2 12.1 %scatter_custom_fusion.2 = f32[15,4096]{0,1:T(8,128)S(1)} fusion(s32[2048]{0:T(1024)} %bitcast.97, f32[2048,15]{1,0:T(8,128)S(1)} %bitcast.77, f32[]{:T(128)} %constant.26.clone.1), kind=kCustom, calls=%fused_computation.12 | custom fusion | flops 30720 | bytes 246272 | tf_op jit(solution)/shard_map/scatter-add | solution.py:93
  443.3 0.8 copy.97
  444.2 0.5 reshape.309
  444.7 20.6 %all_to_all.49 = f32[128,1,480]{2,1,0:T(1,128)S(1)} all-to-all(f32[128,1,480]{2,1,0:T(1,128)S(1)} %reshape.309), channel_id=1, replica_groups=mesh['land'=128,'cam'=4] {'land'}, dimensions={0} | all-to-all | bytes 491520 | tf_op jit(solution)/shard_map/all_to_all | solution.py:95
  465.3 1.2 reduce.9
  466.8 0.3 copy.98
  467.1 0.5 reshape.270
  467.6 0.6 copy.99
  468.2 22.6 %scatter_custom_fusion.3 = f32[15,1024]{0,1:T(8,128)S(1)} fusion(s32[4096]{0:T(1024)} %bitcast.92, f32[4096,15]{1,0:T(8,128)S(1)} %copy.99, f32[]{:T(128)} %constant.26.clone.1), kind=kCustom, calls=%fused_computation.16 | custom fusion | flops 61440 | bytes 61952 | tf_op jit(solution)/shard_map/scatter-add | solution.py:98
  490.9 0.8 copy.100
  491.7 15.1 %reduce-scatter.5.cloned.1.call-done = f32[15,256]{1,0:T(8,128)} async-done(((f32[15,1024]{1,0:T(8,128)}), f32[15,256]{1,0:T(8,128)}) %reduce-scatter.5.cloned.1.call-update) | async-done | bytes 15376 | tf_op jit(solution)/shard_map/reduce_scatter | solution.py:97
  506.8 1.3 multiply_reduce_fusion.10
  508.1 99.5 %psum.31 = f32[1]{0:T(128)} all-reduce(f32[1]{0:T(128)} %bitcast.34), channel_id=1, replica_groups=mesh['land'=128,'cam'=4] {'land','cam'}, use_global_device_ids=true, to_apply=%region_29.32 | all-reduce | flops 1 | bytes 8 | tf_op jit(solution)/shard_map/psum | solution.py:73
  608.9 1.3 multiply_subtract_fusion
  (57 shorter events, 2.5 us)
Async XLA Ops:
  38.5 22.6 %copy-start.5 = (s32[4,512]{1,0:T(4,128)S(1)}, s32[4,512]{1,0:T(4,128)}, u32[]{:S(2)}) copy-start(s32[4,512]{1,0:T(4,128)} %param.16) | copy-start | bytes 24580
  40.6 34.7 %all-to-all-start = ((f32[128,1,480]{2,1,0:T(1,128)}), f32[128,1,480]{2,1,0:T(1,128)S(1)}, u32[]{:S(2)}, u32[]{:S(2)}) async-start(f32[128,1,480]{2,1,0:T(1,128)} %reshape.303), calls=%async_computation | async-start | bytes 524288 | tf_op jit(solution)/shard_map/all_to_all | solution.py:83
  78.1 6.2 %copy-start = (f32[2,15,4,512]{3,2,1,0:T(4,128)S(1)}, f32[2,15,4,512]{3,2,1,0:T(4,128)}, u32[]{:S(2)}) copy-start(f32[2,15,4,512]{3,2,1,0:T(4,128)} %param.13) | copy-start | bytes 737284
  83.6 0.8 copy-start.6
  83.6 0.9 copy-start.11
  98.9 9.3 %copy-start.3 = (s32[1,4096]{1,0:T(1,128)S(1)}, s32[1,4096]{1,0:T(1,128)}, u32[]{:S(2)}) copy-start(s32[1,4096]{1,0:T(1,128)} %param.18) | copy-start | bytes 49156
  101.0 21.3 %all-to-all-start.1 = ((f32[128,1,480]{2,1,0:T(1,128)}), f32[128,1,480]{2,1,0:T(1,128)S(1)}, u32[]{:S(2)}, u32[]{:S(2)}) async-start(f32[128,1,480]{2,1,0:T(1,128)} %reshape.305), calls=%async_computation.1 | async-start | bytes 524288 | tf_op jit(solution)/shard_map/all_to_all | solution.py:95
  108.0 57.4 %reduce-scatter.3.cloned.1.call-start = ((), (), s32[]{:S(2)}) async-start(), calls=%async_computation.6 | async-start | bytes 81920 | tf_op jit(solution)/shard_map/reduce_scatter | solution.py:97
  108.2 17.0 %copy-start.7 = (s32[4096,1]{0,1:T(1,128)}, s32[4096,1]{0,1:T(1,128)S(1)}, u32[]{:S(2)}) copy-start(s32[4096,1]{0,1:T(1,128)S(1)} %compare_select_fusion) | copy-start | bytes 49156
  124.1 41.2 %copy-start.2 = (f32[15,256]{1,0:T(8,128)S(1)}, f32[15,256]{1,0:T(8,128)}, u32[]{:S(2)}) copy-start(f32[15,256]{1,0:T(8,128)} %param.21) | copy-start | bytes 46084
  124.1 41.2 %copy-start.4 = (f32[15,256]{1,0:T(8,128)S(1)}, f32[15,256]{1,0:T(8,128)}, u32[]{:S(2)}) copy-start(f32[15,256]{1,0:T(8,128)} %param.19) | copy-start | bytes 46084
  124.6 143.6 %copy-start.1 = (f32[15,15,256]{2,1,0:T(8,128)S(1)}, f32[15,15,256]{2,1,0:T(8,128)}, u32[]{:S(2)}) copy-start(f32[15,15,256]{2,1,0:T(8,128)} %param.20) | copy-start | bytes 691204
  148.6 358.2 %reduce-scatter.5.cloned.1.call-start = ((), (), s32[]{:S(2)}) async-start(), calls=%async_computation.7 | async-start | bytes 81920 | tf_op jit(solution)/shard_map/reduce_scatter | solution.py:97
  429.8 0.8 copy-start.8
  429.8 0.8 copy-start.9
  429.8 0.8 copy-start.10
Sparse Core Ops, SparseCore 0:
  148.7 16.5 reduce-scatter.2
  491.8 14.9 reduce-scatter.4
where the time goes:
time: 619 us; the launch traced here: 617 us
  blocking collectives  363 us (59%)
  other arithmetic  92.7 us (15%)
  waiting for transfers between devices  58.8 us (9%)
  local copies, waits for them, and re-layouts  55.6 us (9%)
  starting transfers between devices  27.7 us (4%)
  between operations  19.2 us (3%)
    psum x3, blocking collectives, global_dots(): return lax.psum(jnp.stack(terms), ('land', 'cam'))  295 us
    scatter-add x2, other arithmetic, local(): jnp.zeros((PARAMS, group_size), jnp.float32).at[:, targets].add(returned)  45.1 us
    reduce_scatter x2, waiting for transfers between devices, local(): lax.psum_scatter(jnp.zeros((PARAMS, group_size), jnp.float32).at[:, targe...  31.8 us
    gather x2, local copies, waits for them, and re-layouts, local(): outgoing = jnp.take(operate_group_dirs, targets, axis=1)  28.2 us
    all_to_all x1, blocking collectives, local(): lax.all_to_all(outgoing, 'land', split_axis=1, concat_axis=1, tiled=True)  27.7 us
    scatter-add x2, other arithmetic, local(): slot_terms = jnp.zeros((PARAMS, slot_count), jnp.float32).at[:, flat_slot...  24.2 us
    all_to_all x1, blocking collectives, local(): lax.all_to_all(slot_terms, 'land', split_axis=1, concat_axis=1, tiled=True)  20.6 us
    all_to_all x1, starting transfers between devices, local(): lax.all_to_all(outgoing, 'land', split_axis=1, concat_axis=1, tiled=True)  20.5 us
  transfers between devices with their start and end apart: 4, of which 4 were waited for; matrix products, arithmetic and copies ran while one was open for 0% of the time, Pallas kernels for 0%

commit v1 on v0

v1 whole, which is shorter than its diff:
```python
import jax
import jax.numpy as jnp
from jax import lax
from jax.experimental import pallas as pl
from jax.experimental.pallas import tpu as pltpu
from jax.sharding import PartitionSpec as P

MESH = pl.DeviceIdType.MESH
F32 = jnp.float32
BF16 = jnp.bfloat16
PARAMS = 15
N_LAND = 128
N_CAM = 4
NT = (((1,), (1,)), ((), ()))


def split(value):
    head = value.astype(BF16)
    return head, (value - head.astype(F32)).astype(BF16)


def total(value):
    return jnp.sum(jnp.sum(value, axis=1, keepdims=True), axis=0, keepdims=True)


def pick(row, lane):
    lanes = lax.broadcasted_iota(jnp.int32, row.shape, 1)
    return jnp.sum(jnp.where(lanes == lane, row, 0.0), axis=1, keepdims=True)


def scalar_row(scalars, width):
    lanes = lax.broadcasted_iota(jnp.int32, (1, width), 1)
    row = jnp.zeros((1, width), F32)
    for lane, value in enumerate(scalars):
        row = jnp.where(lanes == lane, value, row)
    return row


def put_scalars(chunk, scalars):
    rows = lax.broadcasted_iota(jnp.int32, chunk.shape, 0)
    for m, value in enumerate(scalars):
        chunk = jnp.where(rows == 16 * m + 15, value, chunk)
    return chunk


def take_scalars(chunk, count):
    return [jnp.sum(chunk[16 * m + 15 : 16 * m + 16, :], axis=1, keepdims=True) for m in range(count)]


def place(k):
    return 4 + (1 - 2 * lax.rem(k, 2)) * lax.div(k + 1, 2)


def kernel(
    tiles, jac_cam, jac_land, land_damp, obs_slot, send_list, rhs, precond, cam_damp,
    step_out, residual_out,
    hot_cam, hot_slot, owner_of, listed, entry_of, jac, land, inverse, seen, spread, owned,
    ag, gs, rr, xs, xr,
    land_send, land_recv, cam_send, cam_recv,
):
    me = lax.axis_index("land")
    cam = lax.axis_index("cam")
    me_y, me_z, me_c = lax.div(me, 16), lax.rem(lax.div(me, 2), 8), lax.rem(me, 2)

    def mixed(index):
        return lax.rem(index, 4) * 32 + lax.div(index, 4)

    def each_land_peer(action):
        for total_steps in range(14):
            first = max(0, total_steps - 7)

            def body(ky, carry, total_steps=total_steps):
                y = lax.rem(me_y + place(ky), 8)
                z = lax.rem(me_z + place(total_steps - ky), 8)
                base = y * 16 + z * 2
                action(base + me_c)
                action(base + 1 - me_c)
                return carry

            lax.fori_loop(first, min(7, total_steps) + 1, body, 0)
        action(me + 1 - 2 * me_c)

    def cam_peers():
        return [lax.rem(cam + hop, N_CAM) for hop in (2, 1, 3)]

    barrier = pltpu.get_barrier_semaphore()
    for peer in cam_peers():
        pl.semaphore_signal(barrier, inc=1, device_id={"cam": peer}, device_id_type=MESH)
    each_land_peer(
        lambda peer: pl.semaphore_signal(barrier, inc=1, device_id={"land": peer}, device_id_type=MESH)
    )

    def land_start(n, forward):
        if forward:
            source, target = mixed, me
            own = mixed(me)
        else:
            source, target = (lambda index: index), mixed(me)
            own = me
        xr[n, target] = xs[n, own]

        def send(peer):
            pltpu.make_async_remote_copy(
                src_ref=xs.at[n, source(peer)],
                dst_ref=xr.at[n, target],
                send_sem=land_send.at[n],
                recv_sem=land_recv.at[n],
                device_id={"land": peer},
                device_id_type=MESH,
            ).start()

        each_land_peer(send)

    def land_wait(n, sem):
        rows = pl.ds(0, N_LAND - 1)
        pltpu.make_async_copy(xs.at[n, rows], xr.at[n, rows], sem.at[n]).wait()

    def cam_start(n, source, target):
        for peer in cam_peers():
            pltpu.make_async_remote_copy(
                src_ref=source(peer),
                dst_ref=target,
                send_sem=cam_send.at[n],
                recv_sem=cam_recv.at[n],
                device_id={"cam": peer},
                device_id_type=MESH,
            ).start()

    def cam_wait(n, sem):
        rows = pl.ds(0, N_CAM - 1)
        pltpu.make_async_copy(gs.at[0, rows], rr.at[0, rows], sem.at[n]).wait()

    def precondition(vector):
        result = precond[0] * vector[0:1]
        for b in range(1, PARAMS):
            result = result + precond[b] * vector[b : b + 1]
        return result

    def gather_start(it, direction, scalars):
        ag[it, cam] = jnp.concatenate([direction, scalar_row(scalars, 256)], axis=0)
        return lambda: cam_start(2 * it, lambda peer: ag.at[it, cam], ag.at[it, cam])

    def make_hot_cam():
        listing = jnp.concatenate([send_list[...], jnp.zeros((96, 128), jnp.int32)], axis=0)
        turned = jnp.transpose(listing)
        entries = turned[0:32]
        for i in range(1, 4):
            entries = entries + pltpu.roll(turned[32 * i : 32 * i + 32], 32 * i, 1)
        owner_of[...] = lax.shift_right_logical(entries, 8)
        listed[...] = lax.bitwise_and(entries, 255)
        rows = lax.broadcasted_iota(jnp.int32, (256, 128), 0)
        for e in range(32):
            hot_cam[:, e * 128 : e * 128 + 128] = jnp.where(rows == listed[e : e + 1, :], 1.0, 0.0).astype(BF16)

    def make_hot_slot():
        slots = obs_slot[...]
        group, entry = lax.shift_right_logical(slots, 5), lax.bitwise_and(slots, 31)
        place_of = lax.shift_right_logical(entry, 4) * 128 + group
        entry_of[...] = lax.bitwise_and(entry, 15)
        rows = lax.broadcasted_iota(jnp.int32, (256, 512), 0)
        for k in range(4):
            hot_slot[:, k * 512 : k * 512 + 512] = jnp.where(rows == place_of[k : k + 1, :], 1.0, 0.0).astype(BF16)

    def live_lanes():
        lanes = lax.broadcasted_iota(jnp.int32, (1, 512), 1)
        return jnp.where(lax.shift_right_logical(lanes, 7) < tiles[0], 1.0, 0.0)

    def make_jac():
        live = live_lanes()
        for r in range(2):
            for k in range(4):
                block = jac_cam[r, :, k, :] * live
                jac[r, :, k * 512 : k * 512 + 512] = jnp.concatenate([block, jnp.zeros((1, 512), F32)], axis=0)

    def make_land():
        live = live_lanes()
        for b in range(3):
            land[b] = jnp.concatenate([jac_land[0, b], jac_land[1, b]], axis=0) * live
        blocks = [[None] * 3 for _ in range(3)]
        for b in range(3):
            for d in range(b, 3):
                entry = jnp.sum(land[b] * land[d], axis=0, keepdims=True)
                if b == d:
                    entry = entry + land_damp[b : b + 1, :]
                blocks[b][d] = blocks[d][b] = entry
        adjugate = [[None] * 3 for _ in range(3)]
        for b in range(3):
            for d in range(3):
                b1, b2, d1, d2 = (d + 1) % 3, (d + 2) % 3, (b + 1) % 3, (b + 2) % 3
                adjugate[b][d] = blocks[b1][d1] * blocks[b2][d2] - blocks[b1][d2] * blocks[b2][d1]
        determinant = sum(blocks[0][d] * adjugate[d][0] for d in range(3))
        for b in range(3):
            for d in range(3):
                inverse[3 * b + d : 3 * b + d + 1, :] = adjugate[b][d] / determinant

    def send_listed(n, it, scalars):
        head, tail = split(ag[it].reshape(64, 256))
        both = jnp.concatenate([head, tail], axis=0)
        columns = []
        for pair in range(16):
            product = jnp.dot(both, hot_cam[:, pair * 256 : pair * 256 + 256], preferred_element_type=F32)
            product = product[0:64] + product[64:128]
            for half in range(2):
                e = 2 * pair + half
                owner = owner_of[e : e + 1, :]
                part = product[:, half * 128 : half * 128 + 128]
                chosen = part[0:16]
                for j in range(1, 4):
                    chosen = jnp.where(owner == j, part[16 * j : 16 * j + 16], chosen)
                columns.append(chosen)
        for quarter in range(4):
            chunk = jnp.concatenate(columns[8 * quarter : 8 * quarter + 8], axis=0)
            if quarter == 0:
                chunk = put_scalars(chunk, scalars)
            xs[n, :, quarter, :] = jnp.transpose(chunk)
        land_start(n, True)

    def observed(n, count):
        turned = [jnp.transpose(xr[n, :, quarter, :]) for quarter in range(4)]
        scalars = take_scalars(turned[0], count)
        slots = jnp.concatenate(
            [jnp.concatenate([turned[0], turned[2]], axis=1), jnp.concatenate([turned[1], turned[3]], axis=1)], axis=0
        )
        head, tail = split(slots)
        both = jnp.concatenate([head, tail], axis=0)
        columns = []
        for pair in range(8):
            product = jnp.dot(both, hot_slot[:, pair * 256 : pair * 256 + 256], preferred_element_type=F32)
            product = product[0:256] + product[256:512]
            for half in range(2):
                k, lane = divmod((2 * pair + half) * 128, 512)
                entry = entry_of[k : k + 1, lane : lane + 128]
                part = product[:, half * 128 : half * 128 + 128]
                chosen = part[0:16]
                for e in range(1, 16):
                    chosen = jnp.where(entry == e, part[16 * e : 16 * e + 16], chosen)
                columns.append(chosen)
        return jnp.concatenate(columns, axis=1), scalars

    def eliminate(gathered):
        rows = []
        for r in range(2):
            for k in range(4):
                lanes = slice(k * 512, k * 512 + 512)
                rows.append(jnp.sum(jac[r, :, lanes] * gathered[:, lanes], axis=0, keepdims=True))
        predicted = jnp.concatenate(rows, axis=0)
        land_rhs = [jnp.sum(land[b] * predicted, axis=0, keepdims=True) for b in range(3)]
        misfit = predicted
        for b in range(3):
            step = sum(inverse[3 * b + d : 3 * b + d + 1, :] * land_rhs[d] for d in range(3))
            misfit = misfit - land[b] * step
        terms = []
        for k in range(4):
            lanes = slice(k * 512, k * 512 + 512)
            terms.append(jac[0, :, lanes] * misfit[k : k + 1] + jac[1, :, lanes] * misfit[4 + k : 5 + k])
        return jnp.concatenate(terms, axis=1), total(predicted * misfit)

    def send_terms(n, terms, scalars):
        head = terms.astype(BF16).astype(F32)
        tail = terms - head
        for k in range(4):
            lanes = slice(k * 512, k * 512 + 512)
            entry = entry_of[k : k + 1, :]
            for e in range(16):
                mask = entry == e
                spread[16 * e : 16 * e + 16, lanes] = jnp.where(mask, head[:, lanes], 0.0).astype(BF16)
                spread[256 + 16 * e : 272 + 16 * e, lanes] = jnp.where(mask, tail[:, lanes], 0.0).astype(BF16)
        sums = lax.dot_general(spread[...], hot_slot[...], NT, preferred_element_type=F32)
        sums = sums[0:256] + sums[256:512]
        for quarter in range(4):
            row, lane = 128 * (quarter % 2), 128 * (quarter // 2)
            chunk = sums[row : row + 128, lane : lane + 128]
            if quarter == 0:
                chunk = put_scalars(chunk, scalars)
            xs[n, :, quarter, :] = jnp.transpose(chunk)
        land_start(n, False)

    def group_sums(n, it, count):
        scalars = []
        for quarter in range(4):
            turned = jnp.transpose(xr[n, :, quarter, :])
            if quarter == 0:
                scalars = take_scalars(turned, count)
            head = turned.astype(BF16).astype(F32)
            tail = turned - head
            for e8 in range(8):
                e = 8 * quarter + e8
                lanes = slice(e * 128, e * 128 + 128)
                owner = owner_of[e : e + 1, :]
                for j in range(4):
                    mask = owner == j
                    rows = slice(16 * e8, 16 * e8 + 16)
                    owned[16 * j : 16 * j + 16, lanes] = jnp.where(mask, head[rows], 0.0).astype(BF16)
                    owned[64 + 16 * j : 80 + 16 * j, lanes] = jnp.where(mask, tail[rows], 0.0).astype(BF16)
        sums = lax.dot_general(owned[...], hot_cam[...], NT, preferred_element_type=F32)
        sums = sums[0:64] + sums[64:128]
        if count:
            rows = lax.broadcasted_iota(jnp.int32, sums.shape, 0)
            sums = jnp.where(lax.bitwise_and(rows, 15) == 15, scalar_row(scalars, 256), sums)
        gs[it] = sums.reshape(4, 16, 256)
        rr[it, cam] = gs[it, cam]
        cam_start(2 * it + 1, lambda peer: gs.at[it, peer], rr.at[it, cam])

    def own_sums(it):
        return rr[it, 0] + rr[it, 1] + rr[it, 2] + rr[it, 3]

    start = rhs[...]
    smoothed = precondition(start)
    send = gather_start(0, smoothed, [])
    make_hot_cam()
    pl.semaphore_wait(barrier, N_LAND - 1 + N_CAM - 1)
    send()
    make_hot_slot()
    make_jac()
    cam_wait(0, cam_recv)
    send_listed(0, 0, [])
    make_land()
    energy = total(start * smoothed)
    land_wait(0, land_recv)
    gathered, _ = observed(0, 0)
    seen[...] = gathered
    terms, _ = eliminate(gathered)
    send_terms(1, terms, [])
    land_wait(1, land_recv)
    group_sums(1, 0, 0)
    cam_wait(1, cam_recv)
    product = own_sums(0)[0:PARAMS] + cam_damp[...] * smoothed

    turned = precondition(product)
    scalars = [energy, total(smoothed * product), total(start * turned), total(product * turned)]
    gather_start(1, turned, scalars)()
    cam_wait(2, cam_recv)
    row = ag[1, 0, 15:16] + ag[1, 1, 15:16] + ag[1, 2, 15:16] + ag[1, 3, 15:16]
    send_listed(2, 1, [pick(row, lane) for lane in range(4)])
    land_wait(2, land_recv)
    gathered, (energy, curve, cross, square) = observed(2, 4)
    stride = energy / curve
    energy_new = energy - stride * (cross + curve) + stride * stride * square
    beta = energy_new / energy
    terms, curve = eliminate((1.0 + beta) * seen[...] - stride * gathered)
    residual = start - stride * product
    smoothed_new = smoothed - stride * turned
    direction = smoothed_new + beta * smoothed
    damped = cam_damp[...] * direction
    send_terms(3, terms, [total(residual * smoothed_new), curve + total(damped * direction)])
    land_wait(3, land_recv)
    group_sums(3, 1, 2)
    cam_wait(3, cam_recv)
    sums = own_sums(1)
    energy, curve = pick(sums[15:16], 0), pick(sums[15:16], 1)
    stride_new = energy / curve
    step_out[...] = stride * smoothed + stride_new * direction
    residual_out[...] = residual - stride_new * (sums[0:PARAMS] + damped)
    for n in range(4):
        land_wait(n, land_send)
        cam_wait(n, cam_send)


def local(jac_cam, jac_land, land_damp, obs_slot, tile_count, send_list, rhs, precond, cam_damp):
    vmem = pl.BlockSpec(memory_space=pltpu.VMEM)
    out = jax.ShapeDtypeStruct((PARAMS, 256), F32)
    return pl.pallas_call(
        kernel,
        out_shape=(out, out),
        in_specs=[pl.BlockSpec(memory_space=pltpu.SMEM)] + [vmem] * 8,
        out_specs=(vmem, vmem),
        scratch_shapes=[
            pltpu.VMEM((256, 4096), BF16),
            pltpu.VMEM((256, 2048), BF16),
            pltpu.VMEM((32, 128), jnp.int32),
            pltpu.VMEM((32, 128), jnp.int32),
            pltpu.VMEM((4, 512), jnp.int32),
            pltpu.VMEM((2, 16, 2048), F32),
            pltpu.VMEM((3, 8, 512), F32),
            pltpu.VMEM((9, 512), F32),
            pltpu.VMEM((16, 2048), F32),
            pltpu.VMEM((512, 2048), BF16),
            pltpu.VMEM((128, 4096), BF16),
            pltpu.VMEM((2, 4, 16, 256), F32),
            pltpu.VMEM((2, 4, 16, 256), F32),
            pltpu.VMEM((2, 4, 16, 256), F32),
            pltpu.VMEM((4, N_LAND, 4, 128), F32),
            pltpu.VMEM((4, N_LAND, 4, 128), F32),
            pltpu.SemaphoreType.DMA((4,)),
            pltpu.SemaphoreType.DMA((4,)),
            pltpu.SemaphoreType.DMA((4,)),
            pltpu.SemaphoreType.DMA((4,)),
        ],
        compiler_params=pltpu.CompilerParams(
            collective_id=0, has_side_effects=True, vmem_limit_bytes=48 * 1024 * 1024
        ),
    )(tile_count, jac_cam, jac_land, land_damp, obs_slot, send_list.reshape(32, 128), rhs, precond, cam_damp)


def solution(mesh):
    whole = ("land", "cam")
    return jax.shard_map(
        local,
        mesh=mesh,
        in_specs=(
            P(None, None, None, whole),
            P(None, None, None, whole),
            P(None, whole),
            P(None, whole),
            P(whole),
            P(whole, None),
            P(None, whole),
            P(None, None, whole),
            P(None, whole),
        ),
        out_specs=(P(None, whole), P(None, whole)),
        check_vma=False,
    )
```

time: 619 us -> 88 us (0.14)
  blocking collectives: 363 us -> 0 us
  other arithmetic: 92.7 us -> 0 us
  Pallas kernels: 0 us -> 78.8 us
  waiting for transfers between devices: 58.8 us -> 0 us
  local copies, waits for them, and re-layouts: 55.6 us -> 7.43 us
  starting transfers between devices: 27.7 us -> 0 us
  between operations: 19.2 us -> 1.3 us
    psum x3 -> x0, blocking collectives: 295 us -> none  [global_dots(): return lax.psum(jnp.stack(terms), ('land', 'cam'))]
    pallas_call x0 -> x1, Pallas kernels: none -> 78.8 us  [local(): pl.pallas_call(kernel, out_shape=(out, out), in_specs=[pl.BlockSpec(memor...]
    scatter-add x4 -> x0, other arithmetic: 69.3 us -> none  [the longest x2 45.1 us: local(): jnp.zeros((PARAMS, group_size), jnp.float32).at[:, targets].add(returned)]
    all_to_all x2 -> x0, blocking collectives: 48.3 us -> none  [the longest x1 27.7 us: local(): lax.all_to_all(outgoing, 'land', split_axis=1, concat_axis=1, tiled=True)]
    gather x4 -> x0, local copies, waits for them, and re-layouts: 39.1 us -> none  [the longest x2 28.2 us: local(): outgoing = jnp.take(operate_group_dirs, targets, axis=1)]
    reduce_scatter x2 -> x0, waiting for transfers between devices: 31.8 us -> none  [local(): lax.psum_scatter(jnp.zeros((PARAMS, group_size), jnp.float32).at[:, targe...]
    all_to_all x2 -> x0, starting transfers between devices: 27.4 us -> none  [the longest x1 20.5 us: local(): lax.all_to_all(outgoing, 'land', split_axis=1, concat_axis=1, tiled=True)]
    all_to_all x2 -> x0, waiting for transfers between devices: 26.9 us -> none  [the longest x1 14.1 us: local(): lax.all_to_all(slot_terms, 'land', split_axis=1, concat_axis=1, tiled=True)]
  transfers between devices with their start and end apart: 4 -> 0, of which waited for: 4 -> 0; matrix products, arithmetic and copies ran while one was open for 0% -> 0% of each run, Pallas kernels for 0% -> 0%
where the time goes in v1:
time: 88 us; the launch traced here: 87.5 us
  Pallas kernels  78.8 us (90%)
  local copies, waits for them, and re-layouts  7.43 us (8%)
  between operations  1.3 us (1%)
    pallas_call x1, Pallas kernels, local(): pl.pallas_call(kernel, out_shape=(out, out), in_specs=[pl.BlockSpec(memor...  78.8 us
    unnamed x18, local copies, waits for them, and re-layouts  7.43 us

profile of v1, /device:TPU:1, one launch (start us, length us, event | category | flops | bytes accessed | tf_op | source)
XLA Modules:
  0.0 87.5 jit_solution(6391993496081088275)
XLA Ops:
  1.3 0.0 copy-start
  1.3 0.9 %copy-done = f32[2,15,4,512]{3,2,1,0:T(4,128)S(1)} copy-done((f32[2,15,4,512]{3,2,1,0:T(4,128)S(1)}, f32[2,15,4,512]{3,2,1,0:T(4,128)}, u32[]{:S(2)}) %copy-start) | copy-done | bytes 245784
  2.2 0.0 copy-start.1
  2.2 0.9 %copy-done.1 = f32[15,15,256]{2,1,0:T(8,128)S(1)} copy-done((f32[15,15,256]{2,1,0:T(8,128)S(1)}, f32[15,15,256]{2,1,0:T(8,128)}, u32[]{:S(2)}) %copy-start.1) | copy-done | bytes 230424
  3.2 0.0 copy-start.2
  3.2 0.8 copy-done.2
  4.0 0.0 copy-start.3
  4.0 0.7 copy-done.3
  4.7 0.0 copy-start.4
  4.7 0.7 copy-done.4
  5.4 0.0 copy-start.5
  5.4 0.7 copy-done.5
  6.1 0.0 copy-start.6
  6.1 0.7 copy-done.6
  6.8 0.0 copy-start.7
  6.8 0.7 copy-done.7
  7.5 78.8 %shard_map.104 = (f32[15,256]{1,0:T(8,128)S(1)}, f32[15,256]{1,0:T(8,128)S(1)}) custom-call(s32[1]{0:T(128)S(6)} %copy.13.tiles, f32[2,15,4,512]{3,2,1,0:T(4,128)S(1)} %copy-done, f32[2,3,4,512]{3,2,1,0:T(4,128)S(1)} %copy-done.2, f32[3,512]{1,0:T(4,128)S(1)} %copy-done.6, s32[4,512]{1,0:T(4,128)S(1)} %copy-done.7, s32[32,128]{1,0:T(8,128)S(1)} %bitcast.1, ...), custom_call_target="tpu_custom_call" | custom-call | tf_op jit(solution)/shard_map/pallas_call | solution.py:362
  86.3 0.6 copy.14
  86.9 0.6 copy.15
Async XLA Ops:
  1.3 0.9 %copy-start = (f32[2,15,4,512]{3,2,1,0:T(4,128)S(1)}, f32[2,15,4,512]{3,2,1,0:T(4,128)}, u32[]{:S(2)}) copy-start(f32[2,15,4,512]{3,2,1,0:T(4,128)} %jac_cam.1) | copy-start | bytes 737284
  2.2 0.9 %copy-start.1 = (f32[15,15,256]{2,1,0:T(8,128)S(1)}, f32[15,15,256]{2,1,0:T(8,128)}, u32[]{:S(2)}) copy-start(f32[15,15,256]{2,1,0:T(8,128)} %precond.1) | copy-start | bytes 691204
  3.2 0.8 copy-start.2
  4.0 0.7 copy-start.3
  4.7 0.7 copy-start.4
  5.4 0.7 copy-start.5
  6.1 0.7 copy-start.6
  6.8 0.7 copy-start.7

commit v2 on v1

--- a/solution.py
+++ b/solution.py
@@ -11,7 +11,6 @@
 PARAMS = 15
 N_LAND = 128
 N_CAM = 4
-NT = (((1,), (1,)), ((), ()))
 
 
 def split(value):
@@ -47,16 +46,14 @@
     return [jnp.sum(chunk[16 * m + 15 : 16 * m + 16, :], axis=1, keepdims=True) for m in range(count)]
 
 
-def place(k):
-    return 4 + (1 - 2 * lax.rem(k, 2)) * lax.div(k + 1, 2)
-
-
 def kernel(
-    tiles, jac_cam, jac_land, land_damp, obs_slot, send_list, rhs, precond, cam_damp,
-    step_out, residual_out,
-    hot_cam, hot_slot, owner_of, listed, entry_of, jac, land, inverse, seen, spread, owned,
-    ag, gs, rr, xs, xr,
-    land_send, land_recv, cam_send, cam_recv,
+    tiles_in, jac_cam_in, jac_land_in, land_damp_in, obs_slot_in, send_list_in, rhs_in, precond_in, cam_damp_in,
+    both_out,
+    tiles, jac_cam, jac_land, land_damp, obs_slot, send_list, group_rhs, group_precond, group_damp,
+    hot_cam, hot_slot, hot_cam_t, hot_slot_t, in_owner, in_entry, owner_of, listed, entry_of, slot_place, jac, land, inverse,
+    seen, spread, owned,
+    ag, parts, products, gs, rr, xs, xr,
+    land_send, land_recv, cam_send, cam_recv, fetch_sem,
 ):
     me = lax.axis_index("land")
     cam = lax.axis_index("cam")
@@ -65,23 +62,36 @@
     def mixed(index):
         return lax.rem(index, 4) * 32 + lax.div(index, 4)
 
+    ring = (4, 3, 5, 2, 6, 1, 7, 0)
+    at_y = [lax.rem(me_y + step, 8) * 16 + me_c for step in range(8)]
+    at_z = [lax.rem(me_z + step, 8) * 2 for step in range(8)]
+    other = 1 - 2 * me_c
+
     def each_land_peer(action):
-        for total_steps in range(14):
-            first = max(0, total_steps - 7)
-
-            def body(ky, carry, total_steps=total_steps):
-                y = lax.rem(me_y + place(ky), 8)
-                z = lax.rem(me_z + place(total_steps - ky), 8)
-                base = y * 16 + z * 2
-                action(base + me_c)
-                action(base + 1 - me_c)
-                return carry
-
-            lax.fori_loop(first, min(7, total_steps) + 1, body, 0)
-        action(me + 1 - 2 * me_c)
+        for far in range(14):
+            for k in range(max(0, far - 7), min(7, far) + 1):
+                peer = at_y[ring[k]] + at_z[ring[far - k]]
+                action(peer)
+                action(peer + other)
+        action(me + other)
 
     def cam_peers():
         return [lax.rem(cam + hop, N_CAM) for hop in (2, 1, 3)]
+
+    pairs = (
+        (rhs_in, group_rhs.at[cam]),
+        (precond_in, group_precond.at[cam]),
+        (send_list_in, send_list),
+        (obs_slot_in, obs_slot),
+        (tiles_in, tiles),
+        (jac_cam_in, jac_cam),
+        (jac_land_in, jac_land),
+        (land_damp_in, land_damp),
+        (cam_damp_in, group_damp.at[cam]),
+    )
+    fetches = [pltpu.make_async_copy(source, target, fetch_sem.at[n]) for n, (source, target) in enumerate(pairs)]
+    for fetch in fetches:
+        fetch.start()
 
     barrier = pltpu.get_barrier_semaphore()
     for peer in cam_peers():
@@ -126,19 +136,24 @@
                 device_id_type=MESH,
             ).start()
 
+    cam_buffers = (ag.at[0], parts, rr, group_precond, group_damp, group_rhs)
+
+    def cam_share(n):
+        row = cam_buffers[n].at[cam]
+        cam_start(n, lambda peer: row, row)
+
     def cam_wait(n, sem):
-        rows = pl.ds(0, N_CAM - 1)
-        pltpu.make_async_copy(gs.at[0, rows], rr.at[0, rows], sem.at[n]).wait()
-
-    def precondition(vector):
-        result = precond[0] * vector[0:1]
+        rows = cam_buffers[n].at[pl.ds(0, N_CAM - 1)]
+        pltpu.make_async_copy(rows, rows, sem.at[n]).wait()
+
+    def precondition(owner, vector):
+        result = group_precond[owner, 0] * vector[0:1]
         for b in range(1, PARAMS):
-            result = result + precond[b] * vector[b : b + 1]
+            result = result + group_precond[owner, b] * vector[b : b + 1]
         return result
 
-    def gather_start(it, direction, scalars):
-        ag[it, cam] = jnp.concatenate([direction, scalar_row(scalars, 256)], axis=0)
-        return lambda: cam_start(2 * it, lambda peer: ag.at[it, cam], ag.at[it, cam])
+    def padded(vector):
+        return jnp.concatenate([vector, jnp.zeros((1, 256), F32)], axis=0)
 
     def make_hot_cam():
         listing = jnp.concatenate([send_list[...], jnp.zeros((96, 128), jnp.int32)], axis=0)
@@ -152,6 +167,20 @@
         for e in range(32):
             hot_cam[:, e * 128 : e * 128 + 128] = jnp.where(rows == listed[e : e + 1, :], 1.0, 0.0).astype(BF16)
 
+    def hot_columns(row):
+        column = jnp.transpose(jnp.broadcast_to(row, (128, 128)))
+        lanes = lax.broadcasted_iota(jnp.int32, (128, 128), 1)
+        halves = [jnp.where(lanes + shift == column, 1.0, 0.0) for shift in (0, 128)]
+        return jnp.concatenate(halves, axis=1).astype(BF16)
+
+    def make_cam_masks():
+        for e in range(32):
+            lanes = slice(e * 128, e * 128 + 128)
+            hot_cam_t[lanes, :] = hot_columns(listed[e : e + 1, :])
+            owner = jnp.broadcast_to(owner_of[e : e + 1, :], (16, 128))
+            for j in range(4):
+                in_owner[16 * j : 16 * j + 16, lanes] = jnp.where(owner == j, 1.0, 0.0).astype(BF16)
+
     def make_hot_slot():
         slots = obs_slot[...]
         group, entry = lax.shift_right_logical(slots, 5), lax.bitwise_and(slots, 31)
@@ -160,10 +189,21 @@
         rows = lax.broadcasted_iota(jnp.int32, (256, 512), 0)
         for k in range(4):
             hot_slot[:, k * 512 : k * 512 + 512] = jnp.where(rows == place_of[k : k + 1, :], 1.0, 0.0).astype(BF16)
+            slot_place[k : k + 1, :] = place_of[k : k + 1, :]
+
+    def make_slot_masks():
+        for k in range(4):
+            for part in range(4):
+                lanes = slice(part * 128, part * 128 + 128)
+                both = slice(k * 512 + part * 128, k * 512 + part * 128 + 128)
+                hot_slot_t[both, :] = hot_columns(slot_place[k : k + 1, lanes])
+                entry = jnp.broadcast_to(entry_of[k : k + 1, lanes], (16, 128))
+                for e in range(16):
+                    in_entry[16 * e : 16 * e + 16, both] = jnp.where(entry == e, 1.0, 0.0).astype(BF16)
 
     def live_lanes():
         lanes = lax.broadcasted_iota(jnp.int32, (1, 512), 1)
-        return jnp.where(lax.shift_right_logical(lanes, 7) < tiles[0], 1.0, 0.0)
+        return jnp.where(lax.shift_right_logical(lanes, 7) < tiles[...], 1.0, 0.0)
 
     def make_jac():
         live = live_lanes()
@@ -256,16 +296,12 @@
         return jnp.concatenate(terms, axis=1), total(predicted * misfit)
 
     def send_terms(n, terms, scalars):
-        head = terms.astype(BF16).astype(F32)
-        tail = terms - head
-        for k in range(4):
-            lanes = slice(k * 512, k * 512 + 512)
-            entry = entry_of[k : k + 1, :]
-            for e in range(16):
-                mask = entry == e
-                spread[16 * e : 16 * e + 16, lanes] = jnp.where(mask, head[:, lanes], 0.0).astype(BF16)
-                spread[256 + 16 * e : 272 + 16 * e, lanes] = jnp.where(mask, tail[:, lanes], 0.0).astype(BF16)
-        sums = lax.dot_general(spread[...], hot_slot[...], NT, preferred_element_type=F32)
+        head, tail = split(terms)
+        for e in range(16):
+            mask = in_entry[16 * e : 16 * e + 16, :]
+            spread[16 * e : 16 * e + 16, :] = head * mask
+            spread[256 + 16 * e : 272 + 16 * e, :] = tail * mask
+        sums = jnp.dot(spread[...], hot_slot_t[...], preferred_element_type=F32)
         sums = sums[0:256] + sums[256:512]
         for quarter in range(4):
             row, lane = 128 * (quarter % 2), 128 * (quarter // 2)
@@ -275,100 +311,122 @@
             xs[n, :, quarter, :] = jnp.transpose(chunk)
         land_start(n, False)
 
-    def group_sums(n, it, count):
+    def group_sums(n, count):
         scalars = []
         for quarter in range(4):
             turned = jnp.transpose(xr[n, :, quarter, :])
             if quarter == 0:
                 scalars = take_scalars(turned, count)
-            head = turned.astype(BF16).astype(F32)
-            tail = turned - head
+            head, tail = split(turned)
             for e8 in range(8):
-                e = 8 * quarter + e8
-                lanes = slice(e * 128, e * 128 + 128)
-                owner = owner_of[e : e + 1, :]
+                lanes = slice(1024 * quarter + e8 * 128, 1024 * quarter + e8 * 128 + 128)
+                rows = slice(16 * e8, 16 * e8 + 16)
                 for j in range(4):
-                    mask = owner == j
-                    rows = slice(16 * e8, 16 * e8 + 16)
-                    owned[16 * j : 16 * j + 16, lanes] = jnp.where(mask, head[rows], 0.0).astype(BF16)
-                    owned[64 + 16 * j : 80 + 16 * j, lanes] = jnp.where(mask, tail[rows], 0.0).astype(BF16)
-        sums = lax.dot_general(owned[...], hot_cam[...], NT, preferred_element_type=F32)
+                    mask = in_owner[16 * j : 16 * j + 16, lanes]
+                    owned[16 * j : 16 * j + 16, lanes] = head[rows] * mask
+                    owned[64 + 16 * j : 80 + 16 * j, lanes] = tail[rows] * mask
+        sums = jnp.dot(owned[...], hot_cam_t[...], preferred_element_type=F32)
         sums = sums[0:64] + sums[64:128]
         if count:
             rows = lax.broadcasted_iota(jnp.int32, sums.shape, 0)
             sums = jnp.where(lax.bitwise_and(rows, 15) == 15, scalar_row(scalars, 256), sums)
-        gs[it] = sums.reshape(4, 16, 256)
-        rr[it, cam] = gs[it, cam]
-        cam_start(2 * it + 1, lambda peer: gs.at[it, peer], rr.at[it, cam])
-
-    def own_sums(it):
-        return rr[it, 0] + rr[it, 1] + rr[it, 2] + rr[it, 3]
-
-    start = rhs[...]
-    smoothed = precondition(start)
-    send = gather_start(0, smoothed, [])
+        return sums.reshape(4, 16, 256)
+
+    fetches[0].wait()
+    fetches[1].wait()
+    ag[0, cam] = padded(precondition(cam, group_rhs[cam]))
+    pl.semaphore_wait(barrier, N_LAND - 1 + N_CAM - 1)
+    cam_share(0)
+    fetches[2].wait()
     make_hot_cam()
-    pl.semaphore_wait(barrier, N_LAND - 1 + N_CAM - 1)
-    send()
+    for fetch in fetches[3:]:
+        fetch.wait()
     make_hot_slot()
     make_jac()
     cam_wait(0, cam_recv)
     send_listed(0, 0, [])
+    for n in (3, 4, 5):
+        cam_share(n)
     make_land()
-    energy = total(start * smoothed)
+    make_slot_masks()
+    make_cam_masks()
     land_wait(0, land_recv)
     gathered, _ = observed(0, 0)
     seen[...] = gathered
     terms, _ = eliminate(gathered)
     send_terms(1, terms, [])
     land_wait(1, land_recv)
-    group_sums(1, 0, 0)
+    parts[cam] = group_sums(1, 0)
+    cam_share(1)
+    for n in (3, 4, 5):
+        cam_wait(n, cam_recv)
     cam_wait(1, cam_recv)
-    product = own_sums(0)[0:PARAMS] + cam_damp[...] * smoothed
-
-    turned = precondition(product)
-    scalars = [energy, total(smoothed * product), total(start * turned), total(product * turned)]
-    gather_start(1, turned, scalars)()
-    cam_wait(2, cam_recv)
-    row = ag[1, 0, 15:16] + ag[1, 1, 15:16] + ag[1, 2, 15:16] + ag[1, 3, 15:16]
-    send_listed(2, 1, [pick(row, lane) for lane in range(4)])
+
+    sums = [jnp.zeros((PARAMS, 256), F32)] * 4
+    for j in range(N_CAM):
+        start, smoothed = group_rhs[j], ag[0, j, 0:PARAMS]
+        product = parts[0, j, 0:PARAMS] + parts[1, j, 0:PARAMS] + parts[2, j, 0:PARAMS] + parts[3, j, 0:PARAMS]
+        product = product + group_damp[j] * smoothed
+        turned = precondition(j, product)
+        products[j] = product
+        ag[1, j] = padded(turned)
+        pairs = ((start, smoothed), (smoothed, product), (start, turned), (product, turned))
+        sums = [value + left * right for value, (left, right) in zip(sums, pairs)]
+    send_listed(2, 1, [total(value) for value in sums])
     land_wait(2, land_recv)
     gathered, (energy, curve, cross, square) = observed(2, 4)
     stride = energy / curve
     energy_new = energy - stride * (cross + curve) + stride * stride * square
     beta = energy_new / energy
     terms, curve = eliminate((1.0 + beta) * seen[...] - stride * gathered)
-    residual = start - stride * product
-    smoothed_new = smoothed - stride * turned
+    smoothed = ag[0, cam, 0:PARAMS]
+    residual = group_rhs[cam] - stride * products[cam]
+    smoothed_new = smoothed - stride * ag[1, cam, 0:PARAMS]
     direction = smoothed_new + beta * smoothed
-    damped = cam_damp[...] * direction
+    damped = group_damp[cam] * direction
     send_terms(3, terms, [total(residual * smoothed_new), curve + total(damped * direction)])
     land_wait(3, land_recv)
-    group_sums(3, 1, 2)
-    cam_wait(3, cam_recv)
-    sums = own_sums(1)
+    gs[...] = group_sums(3, 2)
+    rr[cam] = gs[cam]
+    cam_start(2, lambda peer: gs.at[peer], rr.at[cam])
+    cam_wait(2, cam_recv)
+    sums = rr[0] + rr[1] + rr[2] + rr[3]
     energy, curve = pick(sums[15:16], 0), pick(sums[15:16], 1)
     stride_new = energy / curve
-    step_out[...] = stride * smoothed + stride_new * direction
-    residual_out[...] = residual - stride_new * (sums[0:PARAMS] + damped)
+    both_out[0] = stride * smoothed + stride_new * direction
+    both_out[1] = residual - stride_new * (sums[0:PARAMS] + damped)
     for n in range(4):
         land_wait(n, land_send)
+    for n in range(6):
         cam_wait(n, cam_send)
 
 
 def local(jac_cam, jac_land, land_damp, obs_slot, tile_count, send_list, rhs, precond, cam_damp):
     vmem = pl.BlockSpec(memory_space=pltpu.VMEM)
-    out = jax.ShapeDtypeStruct((PARAMS, 256), F32)
-    return pl.pallas_call(
+    both = pl.pallas_call(
         kernel,
-        out_shape=(out, out),
-        in_specs=[pl.BlockSpec(memory_space=pltpu.SMEM)] + [vmem] * 8,
-        out_specs=(vmem, vmem),
+        out_shape=jax.ShapeDtypeStruct((2, PARAMS, 256), F32),
+        in_specs=[pl.BlockSpec(memory_space=pl.ANY)] * 9,
+        out_specs=vmem,
         scratch_shapes=[
+            pltpu.VMEM((1, 1), jnp.int32),
+            pltpu.VMEM((2, PARAMS, 4, 512), F32),
+            pltpu.VMEM((2, 3, 4, 512), F32),
+            pltpu.VMEM((3, 512), F32),
+            pltpu.VMEM((4, 512), jnp.int32),
+            pltpu.VMEM((32, 128), jnp.int32),
+            pltpu.VMEM((N_CAM, PARAMS, 256), F32),
+            pltpu.VMEM((N_CAM, PARAMS, PARAMS, 256), F32),
+            pltpu.VMEM((N_CAM, PARAMS, 256), F32),
             pltpu.VMEM((256, 4096), BF16),
+            pltpu.VMEM((256, 2048), BF16),
+            pltpu.VMEM((4096, 256), BF16),
+            pltpu.VMEM((2048, 256), BF16),
+            pltpu.VMEM((64, 4096), BF16),
             pltpu.VMEM((256, 2048), BF16),
             pltpu.VMEM((32, 128), jnp.int32),
             pltpu.VMEM((32, 128), jnp.int32),
+            pltpu.VMEM((4, 512), jnp.int32),
             pltpu.VMEM((4, 512), jnp.int32),
             pltpu.VMEM((2, 16, 2048), F32),
             pltpu.VMEM((3, 8, 512), F32),
@@ -377,19 +435,23 @@
             pltpu.VMEM((512, 2048), BF16),
             pltpu.VMEM((128, 4096), BF16),
             pltpu.VMEM((2, 4, 16, 256), F32),
-            pltpu.VMEM((2, 4, 16, 256), F32),
-            pltpu.VMEM((2, 4, 16, 256), F32),
+            pltpu.VMEM((N_CAM, N_CAM, 16, 256), F32),
+            pltpu.VMEM((N_CAM, PARAMS, 256), F32),
+            pltpu.VMEM((N_CAM, 16, 256), F32),
+            pltpu.VMEM((N_CAM, 16, 256), F32),
             pltpu.VMEM((4, N_LAND, 4, 128), F32),
             pltpu.VMEM((4, N_LAND, 4, 128), F32),
             pltpu.SemaphoreType.DMA((4,)),
             pltpu.SemaphoreType.DMA((4,)),
-            pltpu.SemaphoreType.DMA((4,)),
-            pltpu.SemaphoreType.DMA((4,)),
+            pltpu.SemaphoreType.DMA((6,)),
+            pltpu.SemaphoreType.DMA((6,)),
+            pltpu.SemaphoreType.DMA((9,)),
         ],
         compiler_params=pltpu.CompilerParams(
-            collective_id=0, has_side_effects=True, vmem_limit_bytes=48 * 1024 * 1024
+            collective_id=0, has_side_effects=True, vmem_limit_bytes=60 * 1024 * 1024
         ),
-    )(tile_count, jac_cam, jac_land, land_damp, obs_slot, send_list.reshape(32, 128), rhs, precond, cam_damp)
+    )(tile_count.reshape(1, 1), jac_cam, jac_land, land_damp, obs_slot, send_list.reshape(32, 128), rhs, precond, cam_damp)
+    return both[0], both[1]
 
 
 def solution(mesh):

time: 88 us -> 78.6 us (0.89)
  local copies, waits for them, and re-layouts: 7.43 us -> 1.35 us
  Pallas kernels: 78.8 us -> 75.8 us
    unnamed x18 -> x0, local copies, waits for them, and re-layouts: 7.43 us -> none
    pallas_call x1, Pallas kernels: 78.8 us -> 75.8 us  [local(): pl.pallas_call(kernel, out_shape=jax.ShapeDtypeStruct((2, PARAMS, 256), F...]
    squeeze x0 -> x1, local copies, waits for them, and re-layouts: none -> 1.35 us  [local(): return (both[0], both[1])]
where the time goes in v2:
time: 78.6 us; the launch traced here: 78.4 us
  Pallas kernels  75.8 us (96%)
  local copies, waits for them, and re-layouts  1.35 us (2%)
  between operations  1.29 us (2%)
    pallas_call x1, Pallas kernels, local(): pl.pallas_call(kernel, out_shape=jax.ShapeDtypeStruct((2, PARAMS, 256), F...  75.8 us

profile of v2, /device:TPU:1, one launch (start us, length us, event | category | flops | bytes accessed | tf_op | source)
XLA Modules:
  0.0 78.4 jit_solution(13826544631052704838)
XLA Ops:
  1.3 75.8 %shard_map.104 = f32[2,15,256]{2,1,0:T(8,128)} custom-call(s32[1,1]{1,0:T(1,128)} %bitcast.6.tiles_in, f32[2,15,4,512]{3,2,1,0:T(4,128)} %jac_cam_in.1, f32[2,3,4,512]{3,2,1,0:T(4,128)} %jac_land_in.1, f32[3,512]{1,0:T(4,128)} %land_damp_in.1, s32[4,512]{1,0:T(4,128)} %obs_slot_in.1, s32[32,128]{1,0:T(8,128)} %bitcast.7, f32[15,256]{1,0:T(8,128)} %rhs_in.1, ...), custom_call_target="tpu_custom_call" | custom-call | tf_op jit(solution)/shard_map/pallas_call | solution.py:406
  77.1 1.3 %slice_bitcast_fusion = (f32[15,256]{1,0:T(8,128)}, f32[15,256]{1,0:T(8,128)}) fusion(f32[2,15,256]{2,1,0:T(8,128)} %shard_map.104), kind=kLoop, calls=%fused_computation | loop fusion | bytes 61440 | tf_op jit(solution)/shard_map/squeeze | solution.py:454

commit v3 on v2

--- a/solution.py
+++ b/solution.py
@@ -51,7 +51,7 @@
     both_out,
     tiles, jac_cam, jac_land, land_damp, obs_slot, send_list, group_rhs, group_precond, group_damp,
     hot_cam, hot_slot, hot_cam_t, hot_slot_t, in_owner, in_entry, owner_of, listed, entry_of, slot_place, jac, land, inverse,
-    seen, spread, owned,
+    seen, owned,
     ag, parts, products, gs, rr, xs, xr,
     land_send, land_recv, cam_send, cam_recv, fetch_sem,
 ):
@@ -262,11 +262,10 @@
             [jnp.concatenate([turned[0], turned[2]], axis=1), jnp.concatenate([turned[1], turned[3]], axis=1)], axis=0
         )
         head, tail = split(slots)
-        both = jnp.concatenate([head, tail], axis=0)
         columns = []
         for pair in range(8):
-            product = jnp.dot(both, hot_slot[:, pair * 256 : pair * 256 + 256], preferred_element_type=F32)
-            product = product[0:256] + product[256:512]
+            hot = hot_slot[:, pair * 256 : pair * 256 + 256]
+            product = jnp.dot(head, hot, preferred_element_type=F32) + jnp.dot(tail, hot, preferred_element_type=F32)
             for half in range(2):
                 k, lane = divmod((2 * pair + half) * 128, 512)
                 entry = entry_of[k : k + 1, lane : lane + 128]
@@ -297,18 +296,22 @@
 
     def send_terms(n, terms, scalars):
         head, tail = split(terms)
-        for e in range(16):
-            mask = in_entry[16 * e : 16 * e + 16, :]
-            spread[16 * e : 16 * e + 16, :] = head * mask
-            spread[256 + 16 * e : 272 + 16 * e, :] = tail * mask
-        sums = jnp.dot(spread[...], hot_slot_t[...], preferred_element_type=F32)
-        sums = sums[0:256] + sums[256:512]
-        for quarter in range(4):
-            row, lane = 128 * (quarter % 2), 128 * (quarter // 2)
-            chunk = sums[row : row + 128, lane : lane + 128]
-            if quarter == 0:
-                chunk = put_scalars(chunk, scalars)
-            xs[n, :, quarter, :] = jnp.transpose(chunk)
+        for half in range(2):
+            sums = jnp.zeros((256, 256), F32)
+            for k in range(4):
+                lanes = slice(k * 512, k * 512 + 512)
+                block = []
+                for part in (head, tail):
+                    for e in range(8 * half, 8 * half + 8):
+                        block.append(part[:, lanes] * in_entry[16 * e : 16 * e + 16, lanes])
+                block = jnp.concatenate(block, axis=0)
+                sums = sums + jnp.dot(block, hot_slot_t[lanes, :], preferred_element_type=F32)
+            sums = sums[0:128] + sums[128:256]
+            for eb in range(2):
+                chunk = sums[:, 128 * eb : 128 * eb + 128]
+                if eb + half == 0:
+                    chunk = put_scalars(chunk, scalars)
+                xs[n, :, half + 2 * eb, :] = jnp.transpose(chunk)
         land_start(n, False)
 
     def group_sums(n, count):
@@ -432,7 +435,6 @@
             pltpu.VMEM((3, 8, 512), F32),
             pltpu.VMEM((9, 512), F32),
             pltpu.VMEM((16, 2048), F32),
-            pltpu.VMEM((512, 2048), BF16),
             pltpu.VMEM((128, 4096), BF16),
             pltpu.VMEM((2, 4, 16, 256), F32),
             pltpu.VMEM((N_CAM, N_CAM, 16, 256), F32),

time: 78.6 us -> 77.7 us (0.989)
  Pallas kernels: 75.8 us -> 74.9 us
    pallas_call x1, Pallas kernels: 75.8 us -> 74.9 us  [local(): pl.pallas_call(kernel, out_shape=jax.ShapeDtypeStruct((2, PARAMS, 256), F...]
where the time goes in v3:
time: 77.7 us; the launch traced here: 77.5 us
  Pallas kernels  74.9 us (96%)
  local copies, waits for them, and re-layouts  1.35 us (2%)
  between operations  1.29 us (2%)
    pallas_call x1, Pallas kernels, local(): pl.pallas_call(kernel, out_shape=jax.ShapeDtypeStruct((2, PARAMS, 256), F...  74.9 us

profile of v3, /device:TPU:1, one launch (start us, length us, event | category | flops | bytes accessed | tf_op | source)
XLA Modules:
  0.0 77.5 jit_solution(2103994259286773653)
XLA Ops:
  1.3 74.9 %shard_map.104 = f32[2,15,256]{2,1,0:T(8,128)} custom-call(s32[1,1]{1,0:T(1,128)} %bitcast.6.tiles_in, f32[2,15,4,512]{3,2,1,0:T(4,128)} %jac_cam_in.1, f32[2,3,4,512]{3,2,1,0:T(4,128)} %jac_land_in.1, f32[3,512]{1,0:T(4,128)} %land_damp_in.1, s32[4,512]{1,0:T(4,128)} %obs_slot_in.1, s32[32,128]{1,0:T(8,128)} %bitcast.7, f32[15,256]{1,0:T(8,128)} %rhs_in.1, ...), custom_call_target="tpu_custom_call" | custom-call | tf_op jit(solution)/shard_map/pallas_call | solution.py:409
  76.2 1.3 %slice_bitcast_fusion = (f32[15,256]{1,0:T(8,128)}, f32[15,256]{1,0:T(8,128)}) fusion(f32[2,15,256]{2,1,0:T(8,128)} %shard_map.104), kind=kLoop, calls=%fused_computation | loop fusion | bytes 61440 | tf_op jit(solution)/shard_map/squeeze | solution.py:456

commit v4 on v3

--- a/solution.py
+++ b/solution.py
@@ -51,7 +51,7 @@
     both_out,
     tiles, jac_cam, jac_land, land_damp, obs_slot, send_list, group_rhs, group_precond, group_damp,
     hot_cam, hot_slot, hot_cam_t, hot_slot_t, in_owner, in_entry, owner_of, listed, entry_of, slot_place, jac, land, inverse,
-    seen, owned,
+    seen,
     ag, parts, products, gs, rr, xs, xr,
     land_send, land_recv, cam_send, cam_recv, fetch_sem,
 ):
@@ -316,19 +316,18 @@
 
     def group_sums(n, count):
         scalars = []
+        sums = jnp.zeros((128, 256), F32)
         for quarter in range(4):
             turned = jnp.transpose(xr[n, :, quarter, :])
             if quarter == 0:
                 scalars = take_scalars(turned, count)
-            head, tail = split(turned)
-            for e8 in range(8):
-                lanes = slice(1024 * quarter + e8 * 128, 1024 * quarter + e8 * 128 + 128)
-                rows = slice(16 * e8, 16 * e8 + 16)
+            block = []
+            for part in split(turned):
+                row = jnp.concatenate([part[16 * e : 16 * e + 16] for e in range(8)], axis=1)
                 for j in range(4):
-                    mask = in_owner[16 * j : 16 * j + 16, lanes]
-                    owned[16 * j : 16 * j + 16, lanes] = head[rows] * mask
-                    owned[64 + 16 * j : 80 + 16 * j, lanes] = tail[rows] * mask
-        sums = jnp.dot(owned[...], hot_cam_t[...], preferred_element_type=F32)
+                    block.append(row * in_owner[16 * j : 16 * j + 16, 1024 * quarter : 1024 * quarter + 1024])
+            hot = hot_cam_t[1024 * quarter : 1024 * quarter + 1024, :]
+            sums = sums + jnp.dot(jnp.concatenate(block, axis=0), hot, preferred_element_type=F32)
         sums = sums[0:64] + sums[64:128]
         if count:
             rows = lax.broadcasted_iota(jnp.int32, sums.shape, 0)
@@ -435,7 +434,6 @@
             pltpu.VMEM((3, 8, 512), F32),
             pltpu.VMEM((9, 512), F32),
             pltpu.VMEM((16, 2048), F32),
-            pltpu.VMEM((128, 4096), BF16),
             pltpu.VMEM((2, 4, 16, 256), F32),
             pltpu.VMEM((N_CAM, N_CAM, 16, 256), F32),
             pltpu.VMEM((N_CAM, PARAMS, 256), F32),

time: 77.7 us -> 77.4 us (level)
  no operation moved by 1% of the time
where the time goes in v4:
time: 77.4 us; the launch traced here: 77.2 us
  Pallas kernels  74.5 us (96%)
  local copies, waits for them, and re-layouts  1.35 us (2%)
  between operations  1.29 us (2%)
    pallas_call x1, Pallas kernels, local(): pl.pallas_call(kernel, out_shape=jax.ShapeDtypeStruct((2, PARAMS, 256), F...  74.5 us

profile of v4, /device:TPU:1, one launch (start us, length us, event | category | flops | bytes accessed | tf_op | source)
XLA Modules:
  0.0 77.2 jit_solution(1959098098187887348)
XLA Ops:
  1.3 74.5 %shard_map.104 = f32[2,15,256]{2,1,0:T(8,128)} custom-call(s32[1,1]{1,0:T(1,128)} %bitcast.6.tiles_in, f32[2,15,4,512]{3,2,1,0:T(4,128)} %jac_cam_in.1, f32[2,3,4,512]{3,2,1,0:T(4,128)} %jac_land_in.1, f32[3,512]{1,0:T(4,128)} %land_damp_in.1, s32[4,512]{1,0:T(4,128)} %obs_slot_in.1, s32[32,128]{1,0:T(8,128)} %bitcast.7, f32[15,256]{1,0:T(8,128)} %rhs_in.1, ...), custom_call_target="tpu_custom_call" | custom-call | tf_op jit(solution)/shard_map/pallas_call | solution.py:408
  75.8 1.3 %slice_bitcast_fusion = (f32[15,256]{1,0:T(8,128)}, f32[15,256]{1,0:T(8,128)}) fusion(f32[2,15,256]{2,1,0:T(8,128)} %shard_map.104), kind=kLoop, calls=%fused_computation | loop fusion | bytes 61440 | tf_op jit(solution)/shard_map/squeeze | solution.py:454
